TPU v7x, 256 devices: a whole 4x4x8 slice. The times are simulated.
256 devices in a mesh: dp: 8 (over x, core), tensor: 32 (over z, y).
Axes of the slice: x: 4, y: 4, z: 8, core: 2. Of those that a mesh axis runs over, the one named last changes fastest.
Arguments:
- acts: bfloat16 [3072, 8192], P('dp', 'tensor'), may hold values from -6 to 6
- gate_weight: bfloat16 [8192, 16384], P(None, 'tensor'), may hold values from -0.0625 to 0.0625
Outputs:
- covariance: float32 [8192, 8192], P('tensor', 'dp')
- gate_out: bfloat16 [3072, 16384], P('dp', 'tensor')
All inputs are finite; a program needn't handle non-finite values.
Results may differ from a plain program's by a relative error of at most 0.001.
Values may be sent and summed in bfloat16 or wider, within the bound.
A program may use at most 64 MiB of HBM per device.

v0:
```python
import jax
import jax.numpy as jnp
from jax import lax
from jax.sharding import PartitionSpec as P


def outer_sum(left, right):
    return lax.dot_general(
        left, right, (((0,), (0,)), ((), ())), preferred_element_type=jnp.float32
    )


def shards(acts, gate_weight):
    tok_rows = acts.shape[0]
    token_total = tok_rows * lax.axis_size("dp")
    gathered = lax.all_gather(acts, "tensor", axis=1, tiled=True)
    gate_sum = jnp.dot(gathered, gate_weight, preferred_element_type=jnp.float32)
    columns = lax.all_to_all(gathered, "dp", split_axis=1, concat_axis=0, tiled=True)
    row_panel = lax.all_gather(acts, "dp", axis=0, tiled=True)
    cov_tile = outer_sum(row_panel, columns)
    return (cov_tile / jnp.float32(token_total), gate_sum.astype(jnp.bfloat16))


def solution(mesh):
    return jax.shard_map(
        shards,
        mesh=mesh,
        in_specs=(P("dp", "tensor"), P(None, "tensor")),
        out_specs=(P("tensor", "dp"), P("dp", "tensor")),
        check_vma=False,
    )
```

profile of v0, /device:TPU:4, one launch (start us, length us, event | category | flops | bytes accessed | tf_op | source)
XLA Modules:
  0.0 206.4 jit_solution(3676476535161484212)
XLA Ops:
  8.0 0.0 all-gather.5.cloned.1.call-start
  8.0 1.7 copy.4
  9.8 0.0 all-gather.5.cloned.1.call-update
  9.8 93.9 %all-gather.5.cloned.1.call-done = bf16[384,8192]{0,1:T(8,128)(2,1)} async-done(((bf16[384,256]{0,1:T(8,128)(2,1)}), bf16[384,8192]{0,1:T(8,128)(2,1)}) %all-gather.5.cloned.1.call-update) | async-done | bytes 6291472 | tf_op jit(solution)/shard_map/all_gather | solution.py:16
  103.7 5.2 %all-to-all-start = ((bf16[384,8,1024]{0,2,1:T(8,128)(2,1)}), bf16[384,8,1024]{0,2,1:T(8,128)(2,1)}, u32[]{:S(2)}, u32[]{:S(2)}) async-start(bf16[384,8,1024]{0,2,1:T(8,128)(2,1)} %bitcast.8), calls=%async_computation | async-start | bytes 12582912 | tf_op jit(solution)/shard_map/all_to_all | solution.py:18
  108.9 0.0 all-gather.3.cloned.1.call-start
  108.9 0.6 all-gather.3.cloned.1.call-update
  109.4 9.4 %convolution_convert_fusion = bf16[384,512]{1,0:T(8,128)(2,1)} fusion(bf16[384,8192]{0,1:T(8,128)(2,1)} %all-gather.5.cloned.1.call-done, bf16[8192,512]{1,0:T(8,128)(2,1)} %param.3), kind=kOutput, calls=%fused_computation.1 | convolution fusion | flops 3221422080 | bytes 15073280 | tf_op jit(solution)/shard_map/dot_general | solution.py:17
  118.8 65.4 %all-to-all-done = bf16[384,8,1024]{0,2,1:T(8,128)(2,1)} async-done(((bf16[384,8,1024]{0,2,1:T(8,128)(2,1)}), bf16[384,8,1024]{0,2,1:T(8,128)(2,1)}, u32[]{:S(2)}, u32[]{:S(2)}) %all-to-all-start) | async-done | bytes 6291488 | tf_op jit(solution)/shard_map/all_to_all | solution.py:18
  184.3 8.6 %copy.5 = bf16[8,384,1024]{2,1,0:T(8,128)(2,1)} copy(bf16[8,384,1024]{1,2,0:T(8,128)(2,1)} %bitcast.1) | data formatting | bytes 12582912 | tf_op jit(solution)/shard_map/all_to_all | solution.py:18
  192.9 0.0 all-gather.3.cloned.1.call-done
  192.9 6.1 %convolution_multiply_fusion = f32[256,1024]{1,0:T(8,128)} fusion(bf16[3072,256]{1,0:T(8,128)(2,1)} %all-gather.3.cloned.1.call-done, bf16[3072,1024]{1,0:T(8,128)(2,1)} %bitcast.7), kind=kOutput, calls=%fused_computation | convolution fusion | flops 1610874880 | bytes 8912896 | tf_op jit(solution)/shard_map/dot_general | solution.py:8
Async XLA Ops:
  8.0 95.7 %all-gather.5.cloned.1.call-start = ((), (), s32[]{:S(2)}) async-start(), calls=%async_computation.2 | async-start | bytes 6488064 | tf_op jit(solution)/shard_map/all_gather | solution.py:16
  103.7 80.6 %all-to-all-start = ((bf16[384,8,1024]{0,2,1:T(8,128)(2,1)}), bf16[384,8,1024]{0,2,1:T(8,128)(2,1)}, u32[]{:S(2)}, u32[]{:S(2)}) async-start(bf16[384,8,1024]{0,2,1:T(8,128)(2,1)} %bitcast.8), calls=%async_computation | async-start | bytes 12582912 | tf_op jit(solution)/shard_map/all_to_all | solution.py:18
  108.9 84.0 %all-gather.3.cloned.1.call-start = ((), (), s32[]{:S(2)}) async-start(), calls=%async_computation.1 | async-start | bytes 1769472 | tf_op jit(solution)/shard_map/all_gather | solution.py:19
Sparse Core Ops, SparseCore 0:
  12.0 91.6 all-gather.4
Sparse Core Ops, SparseCore 1:
  111.2 27.5 all-gather.2
where the time goes:
time: 210 us; the launch traced here: 206 us
  waiting for transfers between devices  160 us (76%)
  between operations  15.5 us (7%)
  matrix products  15.4 us (7%)
  local copies, waits for them, and re-layouts  10.4 us (5%)
  starting transfers between devices  5.23 us (2%)
    all_gather x1, waiting for transfers between devices, shards(): gathered = lax.all_gather(acts, 'tensor', axis=1, tiled=True)  93.9 us
    all_to_all x1, waiting for transfers between devices, shards(): lax.all_to_all(gathered, 'dp', split_axis=1, concat_axis=0, tiled=True)  65.4 us
    dot_general x1, matrix products, shards(): jnp.dot(gathered, gate_weight, preferred_element_type=jnp.float32)  9.38 us
    all_to_all x1, local copies, waits for them, and re-layouts, shards(): lax.all_to_all(gathered, 'dp', split_axis=1, concat_axis=0, tiled=True)  8.63 us
    dot_general x1, matrix products, outer_sum(): lax.dot_general(left, right, (((0,), (0,)), ((), ())), preferred_element_...  6.06 us
    all_to_all x1, starting transfers between devices, shards(): lax.all_to_all(gathered, 'dp', split_axis=1, concat_axis=0, tiled=True)  5.19 us
  transfers between devices with their start and end apart: 3, of which 2 were waited for; matrix products, arithmetic and copies ran while one was open for 9% of the time, Pallas kernels for 0%

commit v1 on v0

v1 whole, which is shorter than its diff:
```python
import functools

import jax
import jax.numpy as jnp
from jax import lax
from jax.experimental import pallas as pl
from jax.experimental.pallas import tpu as pltpu
from jax.sharding import PartitionSpec as P

MESH = pl.DeviceIdType.MESH

ORDER = (
    (0, 0), (-1, 0), (0, -1), (0, 1), (1, 0), (0, -2), (0, 2), (1, 1),
    (1, -1), (0, -3), (0, 3), (1, 2), (2, 0), (1, -2), (0, 4), (-1, -1),
    (-1, 1), (1, 3), (1, -3), (2, -1), (-1, -2), (-1, 2), (1, 4), (-1, -3),
    (-1, 3), (2, -2), (2, 2), (2, -3), (2, 1), (-1, 4), (2, 3), (2, 4),
)

SENDS = (
    (-1, 0, 1, 0, 0, 2), (-1, 1, 1, 0, 0, 2), (-1, 2, 0, 0, 0, 2), (-1, 3, 0, 0, 0, 2),
    (-1, 2, 1, 0, 0, 2), (-1, 3, 1, 0, 0, 2), (-1, 0, 0, 0, 0, 2), (-1, 1, 0, 0, 0, 2),
    (1, 2, 0, 0, -1, 2), (1, 3, 0, 0, 1, 2), (1, 0, 1, -1, 0, 0), (1, 1, 1, 1, 0, 1),
    (2, 0, 1, 0, 1, 2), (2, 2, 1, 0, -1, 2), (2, 3, 1, 0, 1, 2), (2, 1, 1, 0, -1, 2),
    (2, 0, 1, 0, -1, 2), (2, 1, 0, 1, 0, 1), (2, 3, 0, 1, 0, 2), (2, 1, 1, 0, 1, 2),
    (3, 2, 0, 1, 0, 2), (4, 2, 0, 0, -2, 2), (4, 3, 0, 0, 2, 2), (6, 0, 1, -1, 1, 0),
    (6, 1, 1, 0, 2, 2), (6, 2, 1, 0, -2, 2), (6, 3, 1, 0, 2, 2), (6, 0, 1, 0, -2, 2),
    (7, 1, 1, 0, -2, 2), (7, 2, 0, 0, -3, 0), (7, 3, 0, 1, 1, 2), (7, 0, 0, -1, 0, 0),
    (7, 0, 1, -1, -1, 0), (7, 0, 1, 0, 2, 2), (7, 1, 1, 1, -1, 1), (8, 2, 0, 1, -1, 2),
    (8, 3, 0, 0, 3, 1), (9, 2, 0, -1, 0, 2), (9, 3, 0, -1, 0, 2), (10, 2, 1, 0, -3, 0),
    (10, 3, 1, 0, 3, 1), (10, 1, 1, 0, 3, 2), (10, 0, 1, 0, -3, 2), (11, 1, 1, 0, -3, 2),
    (12, 3, 0, 1, 2, 2), (12, 2, 0, 2, 0, 2), (12, 3, 0, 2, 0, 2), (13, 2, 0, 1, -2, 2),
    (14, 0, 1, 0, 4, 2), (14, 1, 1, 0, 4, 2), (16, 2, 0, -1, -1, 2), (16, 3, 0, -1, 1, 2),
    (16, 0, 1, -1, -2, 0), (16, 1, 1, 1, 3, 1), (17, 0, 1, -1, -3, 0), (18, 2, 0, 1, -3, 0),
    (18, 3, 0, 1, 3, 1), (18, 0, 1, 0, 3, 2), (19, 1, 1, 1, -3, 1), (19, 2, 0, 2, -1, 2),
    (19, 3, 0, 2, 1, 2), (20, 1, 1, 1, -2, 1), (20, 0, 1, -1, 4, 0), (20, 0, 1, -1, 2, 0),
    (20, 1, 1, 1, 2, 1), (21, 1, 1, 1, 4, 1), (21, 2, 0, -1, -2, 2), (21, 3, 0, -1, 2, 2),
    (22, 1, 1, 1, 1, 1), (23, 2, 0, 2, -2, 2), (23, 3, 0, 2, 2, 2), (24, 2, 0, -1, -3, 0),
    (24, 3, 0, -1, 3, 1), (24, 0, 1, -1, 3, 0), (26, 2, 0, 2, -3, 0), (26, 3, 0, 2, 3, 1),
)

TOK, FEA, HID = 384, 256, 512
SPLIT = 160
PARTS = ((0, SPLIT), (SPLIT, TOK))
STEPS = len(ORDER)
HALF = FEA // 2
LAG = 4


def landed(send):
    _, link, part, dy, dz, rows = send
    dy += (-1, 1, 0, 0)[link]
    dz += (0, 0, -1, 1)[link]
    return part, (2 if dy == -2 else dy), (4 if dz == -4 else dz), rows


def rows_of(part, rows):
    start, stop = PARTS[part]
    middle = (start + stop) // 2
    lo = middle if rows == 1 else start
    hi = middle if rows == 0 else stop
    return pl.ds(lo, hi - lo)


def needed(part, dy, dz, rows):
    return [
        n
        for n, send in enumerate(SENDS)
        if landed(send)[:3] == (part, dy, dz)
        and (rows == 2 or landed(send)[3] in (2, rows))
    ]


def tree(step, lo, hi, emit):
    if hi - lo == 1:
        emit(lo)
        return
    mid = (lo + hi) // 2
    lax.cond(
        step < mid,
        lambda: tree(step, lo, mid, emit),
        lambda: tree(step, mid, hi, emit),
    )


def pick(step, values):
    out = jnp.int32(values[0])
    for n, value in enumerate(values[1:], 1):
        out = jnp.where(step == n, jnp.int32(value), out)
    return out


def kernel(
    tokens, acts, weight, cov, gate,
    held, own_t, panel, total, part_sum, from_core, through, from_low, from_high,
    ag_send, ag_recv, core_send, core_recv, x_send, thr_recv, low_recv, high_recv, w_sem,
):
    dp, ten = lax.axis_index("dp"), lax.axis_index("tensor")
    x, core = dp // 2, dp % 2
    z, y = ten // 4, ten % 4

    def at(x_, core_, y_, z_):
        return (x_ * 2 + core_, z_ * 4 + y_)

    links = (
        at(x, core, (y + 1) % 4, z),
        at(x, core, (y + 3) % 4, z),
        at(x, core, y, (z + 1) % 8),
        at(x, core, y, (z + 7) % 8),
    )
    other = at(x, 1 - core, y, z)
    x_up = at((x + 1) % 4, core, y, z)
    x_down = at((x + 3) % 4, core, y, z)

    barrier = pltpu.get_barrier_semaphore()
    for device in (*links, other, x_up, x_down):
        pl.semaphore_signal(barrier, inc=1, device_id=device, device_id_type=MESH)

    w_copy = pltpu.make_async_copy(weight, panel, w_sem)
    w_copy.start()

    def block(dy, dz):
        return ((z + dz + 8) % 8) * 4 + (y + dy + 4) % 4

    held[block(0, 0)] = acts[...]
    pl.semaphore_wait(barrier, 7)

    def gather(n):
        _, link, part, dy, dz, rows = SENDS[n]
        ref = held.at[block(dy, dz), rows_of(part, rows)]
        return pltpu.make_async_remote_copy(
            src_ref=ref,
            dst_ref=ref,
            send_sem=ag_send.at[n],
            recv_sem=ag_recv.at[n],
            device_id=links[link],
            device_id_type=MESH,
        )

    def arrived(n):
        part, dy, dz, rows = landed(SENDS[n])
        ref = held.at[block(dy, dz), rows_of(part, rows)]
        pltpu.make_async_remote_copy(
            src_ref=ref,
            dst_ref=ref,
            send_sem=ag_send.at[n],
            recv_sem=ag_recv.at[n],
            device_id=links[SENDS[n][1]],
            device_id_type=MESH,
        ).wait_recv()

    events = [[] for _ in range(STEPS + 1)]
    seen = set()

    def want(step, receives):
        for n in receives:
            if n not in seen:
                seen.add(n)
                events[step + 1].append((arrived, n))

    for step in range(-1, STEPS):
        for n, send in enumerate(SENDS):
            if send[0] == step:
                want(step, needed(*send[2:]))
                events[step + 1].append((lambda m: gather(m).start(), n))
        if step >= 0:
            for part in range(2):
                want(step, needed(part, *ORDER[step], 2))

    def run(step):
        for action, n in events[step + 1]:
            action(n)

    run(-1)
    own_t[...] = acts[...].T
    total[...] = jnp.zeros_like(total)
    w_copy.wait()

    def where(step):
        dy = pick(step, [a for a, _ in ORDER])
        dz = pick(step, [b for _, b in ORDER])
        plane, col = (z + dz + 8) % 8, (y + dy + 4) % 4
        return plane * 4 + col, col, (plane // 2 - x + 4) % 4, plane % 2 == core

    def to_core(step):
        return pltpu.make_async_remote_copy(
            src_ref=part_sum.at[step],
            dst_ref=from_core.at[step],
            send_sem=core_send.at[step],
            recv_sem=core_recv.at[step],
            device_id=other,
            device_id_type=MESH,
        )

    def along_x(step, half, dst, recv_sem, device):
        return pltpu.make_async_remote_copy(
            src_ref=part_sum.at[step, pl.ds(half * HALF, HALF)],
            dst_ref=dst,
            send_sem=x_send.at[2 * step + half],
            recv_sem=recv_sem,
            device_id=device,
            device_id_type=MESH,
        )

    def thr(step, half, side, col, device):
        slot = 4 * side + col
        return along_x(step, half, through.at[slot], thr_recv.at[slot], device)

    def low(step, half, col):
        rows = pl.ds(half * HALF, HALF)
        return along_x(step, half, from_low.at[col, rows], low_recv.at[2 * col + half], x_up)

    def high(step, half, col):
        rows = pl.ds(half * HALF, HALF)
        return along_x(step, half, from_high.at[col, rows], high_recv.at[2 * col + half], x_down)

    def multiply(step):
        k, _, _, mine = where(step)
        part_sum[step] = jnp.dot(own_t[...], held[k], preferred_element_type=jnp.float32)

        @pl.when(jnp.logical_not(mine))
        def _():
            to_core(step).start()

        rows = pl.ds(pl.multiple_of(k * FEA, FEA), FEA)
        total[...] += jnp.dot(held[k], panel[rows, :], preferred_element_type=jnp.float32)

    def join(step):
        _, col, hops, mine = where(step)

        @pl.when(mine)
        def _():
            to_core(step).wait_recv()
            part_sum[step] += from_core[step]

            @pl.when(hops == 2)
            def _():
                thr(step, 0, 0, col, x_up).start()
                thr(step, 1, 1, col, x_down).start()

            @pl.when(hops == 1)
            def _():
                low(step, 1, col).start()

            @pl.when(hops == 3)
            def _():
                high(step, 0, col).start()

    def pass_on(step):
        _, col, hops, mine = where(step)

        @pl.when(mine & (hops == 1))
        def _():
            thr(step, 0, 0, col, x_up).wait_recv()
            part_sum[step, :HALF] += through[col]
            low(step, 0, col).start()

        @pl.when(mine & (hops == 3))
        def _():
            thr(step, 1, 1, col, x_down).wait_recv()
            part_sum[step, HALF:] += through[4 + col]
            high(step, 1, col).start()

    def finish(step):
        _, col, hops, mine = where(step)

        @pl.when(mine & (hops == 0))
        def _():
            for half in range(2):
                low(step, half, col).wait_recv()
                high(step, half, col).wait_recv()
            sums = part_sum[step] + (from_low[col] + from_high[col])
            cov[:, pl.ds(pl.multiple_of(col * FEA, FEA), FEA)] = sums / jnp.float32(tokens)

    def sent(step):
        _, col, hops, mine = where(step)

        @pl.when(jnp.logical_not(mine))
        def _():
            to_core(step).wait_send()

        @pl.when(mine & (hops != 0))
        def _():
            for half in range(2):
                low(step, half, col).wait_send()

    def step_body(step, _):
        @pl.when(step < STEPS)
        def _():
            tree(step, 0, STEPS, run)
            multiply(step)

        @pl.when((step >= 1) & (step < STEPS + 1))
        def _():
            join(step - 1)

        @pl.when(step >= LAG)
        def _():
            pass_on(step - LAG)

        return 0

    lax.fori_loop(0, STEPS + LAG, step_body, 0)
    gate[...] = total[...].astype(gate.dtype)

    def last_body(step, _):
        finish(step)
        return 0

    def sent_body(step, _):
        sent(step)
        return 0

    lax.fori_loop(0, STEPS, last_body, 0)
    lax.fori_loop(0, STEPS, sent_body, 0)
    for n in range(len(SENDS)):
        gather(n).wait_send()


def solution(mesh):
    def step(acts, weight):
        tokens = acts.shape[0] * mesh.shape["dp"]
        sems = pltpu.SemaphoreType.DMA
        f32, bf16 = jnp.float32, jnp.bfloat16
        return pl.pallas_call(
            functools.partial(kernel, tokens),
            out_shape=(
                jax.ShapeDtypeStruct((FEA, 4 * FEA), f32),
                jax.ShapeDtypeStruct((TOK, HID), bf16),
            ),
            in_specs=[
                pl.BlockSpec(memory_space=pltpu.VMEM),
                pl.BlockSpec(memory_space=pl.ANY),
            ],
            out_specs=[pl.BlockSpec(memory_space=pltpu.VMEM)] * 2,
            scratch_shapes=[
                pltpu.VMEM((32, TOK, FEA), bf16),
                pltpu.VMEM((FEA, TOK), bf16),
                pltpu.VMEM((32 * FEA, HID), bf16),
                pltpu.VMEM((TOK, HID), f32),
                pltpu.VMEM((STEPS, FEA, FEA), f32),
                pltpu.VMEM((STEPS, FEA, FEA), f32),
                pltpu.VMEM((8, HALF, FEA), f32),
                pltpu.VMEM((4, FEA, FEA), f32),
                pltpu.VMEM((4, FEA, FEA), f32),
                sems((len(SENDS),)),
                sems((len(SENDS),)),
                sems((STEPS,)),
                sems((STEPS,)),
                sems((2 * STEPS,)),
                sems((8,)),
                sems((8,)),
                sems((8,)),
                sems(()),
            ],
            compiler_params=pltpu.CompilerParams(
                collective_id=0, has_side_effects=True, vmem_limit_bytes=56 * 2**20
            ),
        )(acts, weight)

    return jax.shard_map(
        step,
        mesh=mesh,
        in_specs=(P("dp", "tensor"), P(None, "tensor")),
        out_specs=(P("tensor", "dp"), P("dp", "tensor")),
        check_vma=False,
    )
```

time: 210 us -> 84.3 us (0.40); the launches traced: 206 us -> 84 us
  waiting for transfers between devices: 160 us -> 0 us
  Pallas kernels: 0 us -> 79.3 us
  matrix products: 15.4 us -> 0 us
  between operations: 15.5 us -> 0.64 us
  local copies, waits for them, and re-layouts: 10.4 us -> 4.07 us
  starting transfers between devices: 5.23 us -> 0 us
    all_gather x2 -> x0, waiting for transfers between devices: 93.9 us -> none  [the longest x1 93.9 us: shards(): gathered = lax.all_gather(acts, 'tensor', axis=1, tiled=True)]
    pallas_call x0 -> x1, Pallas kernels: none -> 79.3 us  [step(): pl.pallas_call(functools.partial(kernel, tokens), out_shape=(jax.ShapeDty...]
    all_to_all x1 -> x0, waiting for transfers between devices: 65.4 us -> none  [shards(): lax.all_to_all(gathered, 'dp', split_axis=1, concat_axis=0, tiled=True)]
    dot_general x2 -> x0, matrix products: 15.4 us -> none  [the longest x1 9.38 us: shards(): jnp.dot(gathered, gate_weight, preferred_element_type=jnp.float32)]
    all_to_all x1 -> x0, local copies, waits for them, and re-layouts: 8.63 us -> none  [shards(): lax.all_to_all(gathered, 'dp', split_axis=1, concat_axis=0, tiled=True)]
    all_to_all x1 -> x0, starting transfers between devices: 5.19 us -> none  [shards(): lax.all_to_all(gathered, 'dp', split_axis=1, concat_axis=0, tiled=True)]
    unnamed x1 -> x2, local copies, waits for them, and re-layouts: 1.74 us -> 4.07 us
  transfers between devices with their start and end apart: 3 -> 0, of which waited for: 2 -> 0; matrix products, arithmetic and copies ran while one was open for 9% -> 0% of each run, Pallas kernels for 0% -> 0%
where the time goes in v1:
time: 84.3 us; the launch traced here: 84 us
  Pallas kernels  79.3 us (94%)
  local copies, waits for them, and re-layouts  4.07 us (5%)
    pallas_call x1, Pallas kernels, step(): pl.pallas_call(functools.partial(kernel, tokens), out_shape=(jax.ShapeDty...  79.3 us
    unnamed x2, local copies, waits for them, and re-layouts  4.07 us

profile of v1, /device:TPU:4, one launch (start us, length us, event | category | flops | bytes accessed | tf_op | source)
XLA Modules:
  0.0 84.0 jit_solution(11037741402930703143)
XLA Ops:
  0.6 79.3 %shard_map.41 = (f32[256,1024]{1,0:T(8,128)}, bf16[384,512]{1,0:T(8,128)(2,1)}) custom-call(bf16[384,256]{1,0:T(8,128)(2,1)} %acts.1, bf16[8192,512]{1,0:T(8,128)(2,1)} %weight.1), custom_call_target="tpu_custom_call" | custom-call | tf_op jit(solution)/shard_map/pallas_call | solution.py:324
  80.0 2.3 %copy.6 = f32[256,1024]{1,0:T(8,128)} copy(f32[256,1024]{1,0:T(8,128)} %get-tuple-element.4) | data formatting | bytes 2097152
  82.3 1.8 %copy.7 = bf16[384,512]{1,0:T(8,128)(2,1)} copy(bf16[384,512]{1,0:T(8,128)(2,1)} %get-tuple-element.5) | data formatting | bytes 786432

commit v2 on v1

v2 whole, which is shorter than its diff:
```python
import functools

import jax
import jax.numpy as jnp
from jax import lax
from jax.experimental import pallas as pl
from jax.experimental.pallas import tpu as pltpu
from jax.sharding import PartitionSpec as P

MESH = pl.DeviceIdType.MESH

ORDER = (
    (0, 0), (-1, 0), (0, -1), (0, 1), (1, 0), (-1, 1), (-1, -1), (0, -2),
    (0, 2), (-1, 2), (-1, -2), (0, -3), (0, 3), (1, 1), (1, -1), (0, 4),
    (-1, 3), (-1, -3), (1, -2), (1, 2), (2, 1), (-1, 4), (2, -1), (1, 3),
    (1, -3), (2, 2), (2, 0), (1, 4), (2, -2), (2, -3), (2, 3), (2, 4),
)

SENDS = (
    (-1, 0, 0, 0, 0, 2), (-1, 1, 0, 0, 0, 2), (-1, 2, 0, 0, 0, 2), (-1, 3, 1, 0, 0, 2),
    (-1, 0, 1, 0, 0, 2), (-1, 1, 1, 0, 0, 2), (-1, 2, 1, 0, 0, 2), (-1, 3, 0, 0, 0, 2),
    (1, 0, 0, -1, 0, 0), (1, 1, 0, 1, 0, 1), (1, 2, 0, -1, 0, 2), (1, 3, 0, -1, 0, 2),
    (1, 2, 0, 0, -1, 2), (1, 0, 1, 0, 1, 2), (1, 1, 1, 0, 1, 2), (1, 3, 1, 0, 1, 2),
    (2, 0, 1, 0, -1, 2), (2, 1, 1, 0, -1, 2), (2, 2, 1, 0, -1, 2), (3, 3, 0, 0, 1, 2),
    (4, 3, 0, -1, 1, 2), (5, 2, 0, -1, -1, 2), (5, 0, 1, -1, 1, 0), (5, 1, 1, 1, 1, 1),
    (6, 2, 0, 0, -2, 2), (6, 0, 1, 0, 2, 2), (6, 1, 1, 0, 2, 2), (6, 3, 1, 0, 2, 2),
    (7, 0, 1, 0, -2, 2), (7, 1, 1, 0, -2, 2), (7, 2, 1, 0, -2, 2), (8, 3, 0, 1, 0, 2),
    (9, 3, 0, 0, 2, 2), (9, 2, 0, 0, -3, 0), (9, 2, 0, 1, 0, 2), (10, 0, 1, -1, 2, 0),
    (10, 1, 1, 1, 2, 1), (10, 0, 1, 0, 3, 2), (10, 1, 1, 0, 3, 2), (10, 3, 1, 0, 3, 1),
    (10, 1, 1, 1, 0, 1), (10, 2, 0, -1, -2, 2), (10, 3, 0, -1, 2, 2), (11, 2, 1, 0, -3, 0),
    (11, 0, 1, 0, -3, 2), (11, 1, 1, 1, -2, 1), (11, 3, 0, 0, 3, 1), (12, 0, 1, -1, -1, 0),
    (13, 3, 0, 1, 1, 2), (13, 2, 0, 2, 0, 2), (13, 3, 0, 2, 0, 2), (14, 2, 0, 1, -1, 2),
    (15, 1, 1, 1, 3, 1), (15, 0, 1, 0, 4, 2), (15, 1, 1, 0, 4, 2), (16, 1, 1, 1, -1, 1),
    (17, 2, 0, -1, -3, 0), (17, 3, 0, -1, 3, 1), (17, 0, 1, -1, 3, 0), (17, 1, 1, 0, -3, 2),
    (17, 0, 1, -1, -3, 0), (19, 2, 0, 1, -2, 2), (19, 3, 0, 1, 2, 2), (20, 0, 1, -1, 0, 0),
    (21, 2, 0, 2, -1, 2), (21, 3, 0, 2, 1, 2), (21, 0, 1, -1, -2, 0), (21, 0, 1, -1, 4, 0),
    (21, 1, 1, 1, 4, 1), (23, 2, 0, 1, -3, 0), (23, 3, 0, 1, 3, 1), (25, 1, 1, 1, -3, 1),
    (25, 2, 0, 2, -2, 2), (25, 3, 0, 2, 2, 2), (29, 2, 0, 2, -3, 0), (29, 3, 0, 2, 3, 1),
)

TOK, FEA, HID = 384, 256, 512
SPLIT = 160
PARTS = ((0, SPLIT), (SPLIT, TOK))
STEPS = len(ORDER)
HALF = FEA // 2
LAG = 8
GATE_LAG = 8
END_LAG = 15
CODED = HALF + HALF // 2


def landed(send):
    _, link, part, dy, dz, rows = send
    dy += (-1, 1, 0, 0)[link]
    dz += (0, 0, -1, 1)[link]
    return part, (2 if dy == -2 else dy), (4 if dz == -4 else dz), rows


def rows_of(part, rows):
    start, stop = PARTS[part]
    middle = (start + stop) // 2
    lo = middle if rows == 1 else start
    hi = middle if rows == 0 else stop
    return pl.ds(lo, hi - lo)


def needed(part, dy, dz, rows):
    return [
        n
        for n, send in enumerate(SENDS)
        if landed(send)[:3] == (part, dy, dz)
        and (rows == 2 or landed(send)[3] in (2, rows))
    ]


def tree(step, lo, hi, emit):
    if hi - lo == 1:
        emit(lo)
        return
    mid = (lo + hi) // 2
    lax.cond(
        step < mid,
        lambda: tree(step, lo, mid, emit),
        lambda: tree(step, mid, hi, emit),
    )


def pick(step, values):
    out = jnp.int32(values[0])
    for n, value in enumerate(values[1:], 1):
        out = jnp.where(step == n, jnp.int32(value), out)
    return out


def encode(sums, ref):
    head = sums.astype(jnp.bfloat16)
    wide = head.astype(jnp.float32)
    usable = jnp.abs(wide) > 1e-37
    inverse = pl.reciprocal(jnp.where(usable, wide, 1.0), approx=True)
    ratio = jnp.where(usable, (sums - wide) * inverse, 0.0)
    level = jnp.clip(jnp.floor(ratio * 2048.0 + 8.0), 0.0, 15.0)
    quarter = HALF // 2
    ref[:HALF] = head
    ref[HALF:] = (level[:quarter] * 16.0 + level[quarter:]).astype(jnp.bfloat16)


def decode(ref):
    wide = ref[:HALF].astype(jnp.float32)
    pair = ref[HALF:].astype(jnp.float32)
    upper = jnp.floor(pair * 0.0625)
    level = jnp.concatenate([upper, pair - upper * 16.0], axis=0)
    return wide + wide * ((level - 7.5) * (1.0 / 2048.0))


def kernel(
    tokens, acts, weight, cov, gate,
    held, own_t, panel, total, part_sum, coded, through, from_low, from_high, cov_buf, gate_buf,
    ag_send, ag_recv, core_send, core_recv, x_send, thr_recv, low_recv, high_recv, w_sem, a_sem, out_sem,
):
    dp, ten = lax.axis_index("dp"), lax.axis_index("tensor")
    x, core = dp // 2, dp % 2
    z, y = ten // 4, ten % 4

    def at(x_, core_, y_, z_):
        return (x_ * 2 + core_, z_ * 4 + y_)

    links = (
        at(x, core, (y + 1) % 4, z),
        at(x, core, (y + 3) % 4, z),
        at(x, core, y, (z + 1) % 8),
        at(x, core, y, (z + 7) % 8),
    )
    other = at(x, 1 - core, y, z)
    x_up = at((x + 1) % 4, core, y, z)
    x_down = at((x + 3) % 4, core, y, z)

    def block(dy, dz):
        return ((z + dz + 8) % 8) * 4 + (y + dy + 4) % 4

    own = block(0, 0)
    barrier = pltpu.get_barrier_semaphore()
    for device in (*links, other, x_up, x_down):
        pl.semaphore_signal(barrier, inc=1, device_id=device, device_id_type=MESH)
    a_copy = pltpu.make_async_copy(acts, held.at[own, pl.ds(0, TOK)], a_sem)
    a_copy.start()
    w_copy = pltpu.make_async_copy(weight, panel, w_sem)
    w_copy.start()
    total[...] = jnp.zeros_like(total)
    a_copy.wait()
    pl.semaphore_wait(barrier, 7)

    def gather(n):
        _, link, part, dy, dz, rows = SENDS[n]
        ref = held.at[block(dy, dz), rows_of(part, rows)]
        return pltpu.make_async_remote_copy(
            src_ref=ref,
            dst_ref=ref,
            send_sem=ag_send.at[n],
            recv_sem=ag_recv.at[n],
            device_id=links[link],
            device_id_type=MESH,
        )

    def arrived(n):
        part, dy, dz, rows = landed(SENDS[n])
        ref = held.at[block(dy, dz), rows_of(part, rows)]
        pltpu.make_async_remote_copy(
            src_ref=ref,
            dst_ref=ref,
            send_sem=ag_send.at[n],
            recv_sem=ag_recv.at[n],
            device_id=links[SENDS[n][1]],
            device_id_type=MESH,
        ).wait_recv()

    events = [[] for _ in range(STEPS + 1)]
    seen = set()

    def want(step, receives):
        for n in receives:
            if n not in seen:
                seen.add(n)
                events[step + 1].append((arrived, n))

    for step in range(-1, STEPS):
        for n, send in enumerate(SENDS):
            if send[0] == step:
                want(step, needed(*send[2:]))
                events[step + 1].append((lambda m: gather(m).start(), n))
        if step >= 0:
            for part in range(2):
                want(step, needed(part, *ORDER[step], 2))

    def run(step):
        for action, n in events[step + 1]:
            action(n)

    def where(step):
        dy = pick(step, [a for a, _ in ORDER])
        dz = pick(step, [b for _, b in ORDER])
        plane, col = (z + dz + 8) % 8, (y + dy + 4) % 4
        return plane * 4 + col, col, (plane // 2 - x + 4) % 4, plane % 2 == core

    def to_core(step, k):
        return pltpu.make_async_remote_copy(
            src_ref=held.at[k, pl.ds(0, TOK)],
            dst_ref=held.at[k, pl.ds(TOK, TOK)],
            send_sem=core_send.at[step],
            recv_sem=core_recv.at[step],
            device_id=other,
            device_id_type=MESH,
        )

    def along_x(step, half, dst, recv_sem, device):
        return pltpu.make_async_remote_copy(
            src_ref=coded.at[step, half],
            dst_ref=dst,
            send_sem=x_send.at[2 * step + half],
            recv_sem=recv_sem,
            device_id=device,
            device_id_type=MESH,
        )

    def thr(step, half, side, col, device):
        slot = 4 * side + col
        return along_x(step, half, through.at[slot], thr_recv.at[slot], device)

    def low(step, half, col):
        return along_x(step, half, from_low.at[2 * col + half], low_recv.at[2 * col + half], x_up)

    def high(step, half, col):
        return along_x(step, half, from_high.at[2 * col + half], high_recv.at[2 * col + half], x_down)

    def share(step):
        k, _, _, mine = where(step)

        @pl.when(jnp.logical_not(mine) | (step == 0))
        def _():
            to_core(step, k).start()

    def partial(step):
        k, col, hops, mine = where(step)

        @pl.when(mine)
        def _():
            @pl.when(step > 0)
            def _():
                to_core(step, k).wait_recv()

            part_sum[step] = jnp.dot(own_t[...], held[k], preferred_element_type=jnp.float32)

            @pl.when((hops == 2) | (hops == 3))
            def _():
                encode(part_sum[step, :HALF], coded.at[step, 0])

            @pl.when(hops == 2)
            def _():
                thr(step, 0, 0, col, x_up).start()

            @pl.when(hops == 3)
            def _():
                high(step, 0, col).start()

            @pl.when((hops == 2) | (hops == 1))
            def _():
                encode(part_sum[step, HALF:], coded.at[step, 1])

            @pl.when(hops == 2)
            def _():
                thr(step, 1, 1, col, x_down).start()

            @pl.when(hops == 1)
            def _():
                low(step, 1, col).start()

    def pass_on(step):
        _, col, hops, mine = where(step)

        @pl.when(mine & (hops == 1))
        def _():
            thr(step, 0, 0, col, x_up).wait_recv()
            encode(part_sum[step, :HALF] + decode(through.at[col]), coded.at[step, 0])
            low(step, 0, col).start()

        @pl.when(mine & (hops == 3))
        def _():
            thr(step, 1, 1, col, x_down).wait_recv()
            encode(part_sum[step, HALF:] + decode(through.at[4 + col]), coded.at[step, 1])
            high(step, 1, col).start()

    def project(step):
        k, _, _, _ = where(step)
        rows = pl.ds(pl.multiple_of(k * FEA, FEA), FEA)
        total[...] += jnp.dot(held[k, :TOK], panel[rows, :], preferred_element_type=jnp.float32)

    def out_copy(col):
        columns = pl.ds(pl.multiple_of(col * FEA, FEA), FEA)
        return pltpu.make_async_copy(cov_buf.at[col], cov.at[:, columns], out_sem.at[col])

    def finish(step):
        _, col, hops, mine = where(step)

        @pl.when(mine & (hops == 0))
        def _():
            for half in range(2):
                low(step, half, col).wait_recv()
                high(step, half, col).wait_recv()
                slot = 2 * col + half
                rows = pl.ds(half * HALF, HALF)
                sums = part_sum[step, rows] + (decode(from_low.at[slot]) + decode(from_high.at[slot]))
                cov_buf[col, rows] = sums / jnp.float32(tokens)
            out_copy(col).start()

    def sent(step):
        k, col, hops, mine = where(step)

        @pl.when(jnp.logical_not(mine) | (step == 0))
        def _():
            to_core(step, k).wait_send()

        @pl.when(mine & (hops != 0))
        def _():
            for half in range(2):
                low(step, half, col).wait_send()

    run(-1)
    share(0)
    own_t[:, :TOK] = held[own, :TOK].T
    to_core(0, own).wait_recv()
    own_t[:, TOK:] = held[own, TOK:].T
    w_copy.wait()

    def step_body(step, _):
        @pl.when(step < STEPS)
        def _():
            tree(step, 0, STEPS, run)

        @pl.when((step > 0) & (step < STEPS))
        def _():
            share(step)

        @pl.when((step >= 1) & (step < STEPS + 1))
        def _():
            partial(step - 1)

        @pl.when(step >= LAG)
        def _():
            pass_on(step - LAG)

        @pl.when(step >= GATE_LAG)
        def _():
            project(step - GATE_LAG)

        @pl.when(step >= END_LAG)
        def _():
            finish(step - END_LAG)

        return 0

    lax.fori_loop(0, STEPS + LAG, step_body, 0)
    gate_buf[...] = total[...].astype(gate.dtype)
    gate_copy = pltpu.make_async_copy(gate_buf, gate, a_sem)
    gate_copy.start()

    def last_body(step, _):
        finish(step)
        return 0

    def sent_body(step, _):
        sent(step)
        return 0

    lax.fori_loop(0, STEPS, sent_body, 0)
    for n in range(len(SENDS)):
        gather(n).wait_send()
    lax.fori_loop(STEPS + LAG - END_LAG, STEPS, last_body, 0)
    gate_copy.wait()
    for col in range(4):
        out_copy(col).wait()


def solution(mesh):
    def step(acts, weight):
        tokens = acts.shape[0] * mesh.shape["dp"]
        sems = pltpu.SemaphoreType.DMA
        f32, bf16 = jnp.float32, jnp.bfloat16
        return pl.pallas_call(
            functools.partial(kernel, tokens),
            out_shape=(
                jax.ShapeDtypeStruct((FEA, 4 * FEA), f32),
                jax.ShapeDtypeStruct((TOK, HID), bf16),
            ),
            in_specs=[pl.BlockSpec(memory_space=pl.ANY)] * 2,
            out_specs=[pl.BlockSpec(memory_space=pl.ANY)] * 2,
            scratch_shapes=[
                pltpu.VMEM((32, 2 * TOK, FEA), bf16),
                pltpu.VMEM((FEA, 2 * TOK), bf16),
                pltpu.VMEM((32 * FEA, HID), bf16),
                pltpu.VMEM((TOK, HID), f32),
                pltpu.VMEM((STEPS, FEA, FEA), f32),
                pltpu.VMEM((STEPS, 2, CODED, FEA), bf16),
                pltpu.VMEM((8, CODED, FEA), bf16),
                pltpu.VMEM((8, CODED, FEA), bf16),
                pltpu.VMEM((8, CODED, FEA), bf16),
                pltpu.VMEM((4, FEA, FEA), f32),
                pltpu.VMEM((TOK, HID), bf16),
                sems((len(SENDS),)),
                sems((len(SENDS),)),
                sems((STEPS,)),
                sems((STEPS,)),
                sems((2 * STEPS,)),
                sems((8,)),
                sems((8,)),
                sems((8,)),
                sems(()),
                sems(()),
                sems((4,)),
            ],
            compiler_params=pltpu.CompilerParams(
                collective_id=0, has_side_effects=True, vmem_limit_bytes=56 * 2**20
            ),
        )(acts, weight)

    return jax.shard_map(
        step,
        mesh=mesh,
        in_specs=(P("dp", "tensor"), P(None, "tensor")),
        out_specs=(P("tensor", "dp"), P("dp", "tensor")),
        check_vma=False,
    )
```

time: 84.3 us -> 68.8 us (0.82)
  Pallas kernels: 79.3 us -> 63.9 us
    pallas_call x1, Pallas kernels: 79.3 us -> 63.9 us  [step(): pl.pallas_call(functools.partial(kernel, tokens), out_shape=(jax.ShapeDty...]
where the time goes in v2:
time: 68.8 us; the launch traced here: 68.6 us
  Pallas kernels  63.9 us (93%)
  local copies, waits for them, and re-layouts  4.07 us (6%)
    pallas_call x1, Pallas kernels, step(): pl.pallas_call(functools.partial(kernel, tokens), out_shape=(jax.ShapeDty...  63.9 us
    unnamed x2, local copies, waits for them, and re-layouts  4.07 us

profile of v2, /device:TPU:4, one launch (start us, length us, event | category | flops | bytes accessed | tf_op | source)
XLA Modules:
  0.0 68.6 jit_solution(12355369469628080313)
XLA Ops:
  0.6 63.9 %shard_map.41 = (f32[256,1024]{1,0:T(8,128)}, bf16[384,512]{1,0:T(8,128)(2,1)}) custom-call(bf16[384,256]{1,0:T(8,128)(2,1)} %acts.1, bf16[8192,512]{1,0:T(8,128)(2,1)} %weight.1), custom_call_target="tpu_custom_call" | custom-call | tf_op jit(solution)/shard_map/pallas_call | solution.py:387
  64.6 2.3 %copy.6 = f32[256,1024]{1,0:T(8,128)} copy(f32[256,1024]{1,0:T(8,128)} %get-tuple-element.4) | data formatting | bytes 2097152
  66.9 1.8 %copy.7 = bf16[384,512]{1,0:T(8,128)(2,1)} copy(bf16[384,512]{1,0:T(8,128)(2,1)} %get-tuple-element.5) | data formatting | bytes 786432

commit v3 on v2

--- a/solution.py
+++ b/solution.py
@@ -10,32 +10,32 @@
 MESH = pl.DeviceIdType.MESH
 
 ORDER = (
-    (0, 0), (-1, 0), (0, -1), (0, 1), (1, 0), (-1, 1), (-1, -1), (0, -2),
-    (0, 2), (-1, 2), (-1, -2), (0, -3), (0, 3), (1, 1), (1, -1), (0, 4),
-    (-1, 3), (-1, -3), (1, -2), (1, 2), (2, 1), (-1, 4), (2, -1), (1, 3),
-    (1, -3), (2, 2), (2, 0), (1, 4), (2, -2), (2, -3), (2, 3), (2, 4),
+    (0, 0), (-1, 0), (0, -1), (0, 1), (1, 0), (1, 1), (1, -1), (-1, 1),
+    (0, -2), (0, 2), (2, 0), (-1, -1), (-1, 2), (0, 3), (-1, -2), (0, -3),
+    (1, -2), (-1, 3), (2, 1), (-1, -3), (1, 2), (0, 4), (2, -2), (2, 2),
+    (1, 3), (1, -3), (-1, 4), (2, -3), (2, 3), (2, -1), (1, 4), (2, 4),
 )
 
 SENDS = (
-    (-1, 0, 0, 0, 0, 2), (-1, 1, 0, 0, 0, 2), (-1, 2, 0, 0, 0, 2), (-1, 3, 1, 0, 0, 2),
-    (-1, 0, 1, 0, 0, 2), (-1, 1, 1, 0, 0, 2), (-1, 2, 1, 0, 0, 2), (-1, 3, 0, 0, 0, 2),
-    (1, 0, 0, -1, 0, 0), (1, 1, 0, 1, 0, 1), (1, 2, 0, -1, 0, 2), (1, 3, 0, -1, 0, 2),
-    (1, 2, 0, 0, -1, 2), (1, 0, 1, 0, 1, 2), (1, 1, 1, 0, 1, 2), (1, 3, 1, 0, 1, 2),
-    (2, 0, 1, 0, -1, 2), (2, 1, 1, 0, -1, 2), (2, 2, 1, 0, -1, 2), (3, 3, 0, 0, 1, 2),
-    (4, 3, 0, -1, 1, 2), (5, 2, 0, -1, -1, 2), (5, 0, 1, -1, 1, 0), (5, 1, 1, 1, 1, 1),
-    (6, 2, 0, 0, -2, 2), (6, 0, 1, 0, 2, 2), (6, 1, 1, 0, 2, 2), (6, 3, 1, 0, 2, 2),
-    (7, 0, 1, 0, -2, 2), (7, 1, 1, 0, -2, 2), (7, 2, 1, 0, -2, 2), (8, 3, 0, 1, 0, 2),
-    (9, 3, 0, 0, 2, 2), (9, 2, 0, 0, -3, 0), (9, 2, 0, 1, 0, 2), (10, 0, 1, -1, 2, 0),
-    (10, 1, 1, 1, 2, 1), (10, 0, 1, 0, 3, 2), (10, 1, 1, 0, 3, 2), (10, 3, 1, 0, 3, 1),
-    (10, 1, 1, 1, 0, 1), (10, 2, 0, -1, -2, 2), (10, 3, 0, -1, 2, 2), (11, 2, 1, 0, -3, 0),
-    (11, 0, 1, 0, -3, 2), (11, 1, 1, 1, -2, 1), (11, 3, 0, 0, 3, 1), (12, 0, 1, -1, -1, 0),
-    (13, 3, 0, 1, 1, 2), (13, 2, 0, 2, 0, 2), (13, 3, 0, 2, 0, 2), (14, 2, 0, 1, -1, 2),
-    (15, 1, 1, 1, 3, 1), (15, 0, 1, 0, 4, 2), (15, 1, 1, 0, 4, 2), (16, 1, 1, 1, -1, 1),
-    (17, 2, 0, -1, -3, 0), (17, 3, 0, -1, 3, 1), (17, 0, 1, -1, 3, 0), (17, 1, 1, 0, -3, 2),
-    (17, 0, 1, -1, -3, 0), (19, 2, 0, 1, -2, 2), (19, 3, 0, 1, 2, 2), (20, 0, 1, -1, 0, 0),
-    (21, 2, 0, 2, -1, 2), (21, 3, 0, 2, 1, 2), (21, 0, 1, -1, -2, 0), (21, 0, 1, -1, 4, 0),
-    (21, 1, 1, 1, 4, 1), (23, 2, 0, 1, -3, 0), (23, 3, 0, 1, 3, 1), (25, 1, 1, 1, -3, 1),
-    (25, 2, 0, 2, -2, 2), (25, 3, 0, 2, 2, 2), (29, 2, 0, 2, -3, 0), (29, 3, 0, 2, 3, 1),
+    (-1, 0, 1, 0, 0, 2), (-1, 1, 0, 0, 0, 2), (-1, 2, 0, 0, 0, 2), (-1, 3, 1, 0, 0, 2),
+    (-1, 1, 1, 0, 0, 2), (-1, 2, 1, 0, 0, 2), (-1, 0, 0, 0, 0, 2), (-1, 3, 0, 0, 0, 2),
+    (1, 1, 0, 1, 0, 1), (1, 2, 0, 0, -1, 2), (1, 3, 0, 1, 0, 2), (1, 2, 0, 1, 0, 2),
+    (1, 0, 1, -1, 0, 0), (1, 1, 1, 0, 1, 2), (1, 3, 1, 0, 1, 2), (1, 0, 1, 0, 1, 2),
+    (2, 1, 1, 0, -1, 2), (2, 2, 1, 0, -1, 2), (2, 0, 1, 0, -1, 2), (2, 3, 0, -1, 0, 2),
+    (3, 1, 1, 1, 0, 1), (3, 3, 0, 0, 1, 2), (5, 2, 0, -1, 0, 2), (5, 0, 0, -1, 0, 0),
+    (6, 2, 0, 1, -1, 2), (6, 1, 1, 0, 2, 2), (6, 3, 1, 0, 2, 2), (6, 0, 1, 0, 2, 2),
+    (6, 0, 1, -1, 1, 0), (6, 1, 1, 1, 1, 1), (7, 1, 1, 1, -1, 1), (7, 3, 0, -1, 1, 2),
+    (7, 2, 1, 0, -2, 2), (7, 0, 1, 0, -2, 2), (10, 3, 0, 0, 2, 2), (10, 1, 1, 0, -2, 2),
+    (10, 2, 0, 0, -2, 2), (12, 1, 1, 1, 2, 1), (12, 2, 0, -1, -1, 2), (12, 3, 1, 0, 3, 1),
+    (12, 0, 1, 0, 3, 2), (12, 2, 0, 2, 0, 2), (12, 3, 0, 2, 0, 2), (13, 1, 1, 0, -3, 2),
+    (13, 0, 1, 0, -3, 2), (13, 3, 0, -1, 2, 2), (13, 3, 0, 1, 1, 2), (14, 2, 0, -1, -2, 2),
+    (14, 0, 1, -1, 2, 0), (15, 1, 1, 0, 3, 2), (15, 2, 1, 0, -3, 0), (15, 0, 1, -1, -2, 0),
+    (15, 3, 0, 0, 3, 1), (16, 2, 0, 0, -3, 0), (16, 1, 1, 1, -2, 1), (17, 0, 1, -1, 3, 0),
+    (18, 2, 0, 2, -1, 2), (18, 1, 1, 1, -3, 1), (18, 3, 0, 2, 1, 2), (19, 0, 1, -1, -3, 0),
+    (19, 2, 0, 1, -2, 2), (19, 2, 0, -1, -3, 0), (20, 3, 0, -1, 3, 1), (21, 3, 0, 1, 2, 2),
+    (22, 1, 1, 0, 4, 2), (22, 0, 1, 0, 4, 2), (22, 0, 1, -1, -1, 0), (22, 1, 1, 1, 3, 1),
+    (22, 2, 0, 2, -2, 2), (22, 3, 0, 2, 2, 2), (25, 3, 0, 1, 3, 1), (26, 2, 0, 1, -3, 0),
+    (26, 1, 1, 1, 4, 1), (26, 0, 1, -1, 4, 0), (27, 2, 0, 2, -3, 0), (27, 3, 0, 2, 3, 1),
 )
 
 TOK, FEA, HID = 384, 256, 512
@@ -43,10 +43,12 @@
 PARTS = ((0, SPLIT), (SPLIT, TOK))
 STEPS = len(ORDER)
 HALF = FEA // 2
-LAG = 8
-GATE_LAG = 8
-END_LAG = 15
-CODED = HALF + HALF // 2
+LAG = 6
+GATE_LAG = 12
+END_LAG = 20
+MOST = max(LAG, GATE_LAG - 3)
+SCALE = 256 * 5.45
+CODED = HALF + HALF // 4
 
 
 def landed(send):
@@ -85,37 +87,54 @@
     )
 
 
-def pick(step, values):
-    out = jnp.int32(values[0])
-    for n, value in enumerate(values[1:], 1):
-        out = jnp.where(step == n, jnp.int32(value), out)
-    return out
+WORDS = tuple(
+    sum((dy + 1 + 4 * (dz + 3)) << (5 * n) for n, (dy, dz) in enumerate(ORDER[w : w + 6]))
+    for w in range(0, STEPS, 6)
+)
+
+
+def offsets(step):
+    word = jnp.int32(WORDS[0])
+    for n, value in enumerate(WORDS[1:], 1):
+        word = jnp.where(step >= 6 * n, jnp.int32(value), word)
+    bits = lax.shift_right_logical(word, 5 * lax.rem(step, 6)) & 31
+    return (bits & 3) - 1, lax.shift_right_logical(bits, 2) - 3
 
 
 def encode(sums, ref):
     head = sums.astype(jnp.bfloat16)
     wide = head.astype(jnp.float32)
-    usable = jnp.abs(wide) > 1e-37
-    inverse = pl.reciprocal(jnp.where(usable, wide, 1.0), approx=True)
-    ratio = jnp.where(usable, (sums - wide) * inverse, 0.0)
-    level = jnp.clip(jnp.floor(ratio * 2048.0 + 8.0), 0.0, 15.0)
-    quarter = HALF // 2
+    inverse = pl.reciprocal(jnp.where(jnp.abs(wide) > 1e-37, wide, 1.0), approx=True)
+    level = jnp.floor(((sums - wide) * SCALE) * inverse + 5.5)
+    q = HALF // 4
+    code = (level[:q] + level[q : 2 * q] * 11.0) + (level[2 * q : 3 * q] * 121.0 + level[3 * q :] * 1331.0)
+    power = jnp.floor(code * (1.0 / 256.0))
+    rest = code - power * 256.0
+    place = jnp.where(rest >= 128.0, -rest, rest + 128.0)
     ref[:HALF] = head
-    ref[HALF:] = (level[:quarter] * 16.0 + level[quarter:]).astype(jnp.bfloat16)
+    ref[HALF:] = (place * jnp.exp2(power)).astype(jnp.bfloat16)
 
 
 def decode(ref):
     wide = ref[:HALF].astype(jnp.float32)
-    pair = ref[HALF:].astype(jnp.float32)
-    upper = jnp.floor(pair * 0.0625)
-    level = jnp.concatenate([upper, pair - upper * 16.0], axis=0)
-    return wide + wide * ((level - 7.5) * (1.0 / 2048.0))
+    place = ref[HALF:].astype(jnp.float32)
+    size = jnp.abs(place)
+    power = jnp.floor(jnp.log2(size * 1.002)) - 7.0
+    size = jnp.floor(size * jnp.exp2(-power) + 0.5)
+    code = power * 256.0 + jnp.where(place < 0.0, size, size - 128.0)
+    one = jnp.floor((code + 0.5) * (1.0 / 1331.0))
+    code = code - one * 1331.0
+    two = jnp.floor((code + 0.5) * (1.0 / 121.0))
+    code = code - two * 121.0
+    three = jnp.floor((code + 0.5) * (1.0 / 11.0))
+    level = jnp.concatenate([code - three * 11.0, three, two, one], axis=0)
+    return wide + wide * ((level - 5.0) * (1.0 / SCALE))
 
 
 def kernel(
     tokens, acts, weight, cov, gate,
-    held, own_t, panel, total, part_sum, coded, through, from_low, from_high, cov_buf, gate_buf,
-    ag_send, ag_recv, core_send, core_recv, x_send, thr_recv, low_recv, high_recv, w_sem, a_sem, out_sem,
+    held, own_t, panel, total, part_sum, coded, through, from_low, from_high,
+    ag_send, ag_recv, core_send, core_recv, x_send, thr_recv, low_recv, high_recv, w_sem, a_sem,
 ):
     dp, ten = lax.axis_index("dp"), lax.axis_index("tensor")
     x, core = dp // 2, dp % 2
@@ -146,14 +165,13 @@
     w_copy = pltpu.make_async_copy(weight, panel, w_sem)
     w_copy.start()
     total[...] = jnp.zeros_like(total)
-    a_copy.wait()
     pl.semaphore_wait(barrier, 7)
 
     def gather(n):
         _, link, part, dy, dz, rows = SENDS[n]
         ref = held.at[block(dy, dz), rows_of(part, rows)]
         return pltpu.make_async_remote_copy(
-            src_ref=ref,
+            src_ref=acts.at[rows_of(part, rows)] if dy == dz == 0 else ref,
             dst_ref=ref,
             send_sem=ag_send.at[n],
             recv_sem=ag_recv.at[n],
@@ -196,10 +214,10 @@
             action(n)
 
     def where(step):
-        dy = pick(step, [a for a, _ in ORDER])
-        dz = pick(step, [b for _, b in ORDER])
-        plane, col = (z + dz + 8) % 8, (y + dy + 4) % 4
-        return plane * 4 + col, col, (plane // 2 - x + 4) % 4, plane % 2 == core
+        dy, dz = offsets(step)
+        plane, col = (z + dz + 8) & 7, (y + dy + 4) & 3
+        hops = (lax.shift_right_logical(plane, 1) - x + 4) & 3
+        return plane * 4 + col, col, hops, (plane & 1) == core
 
     def to_core(step, k):
         return pltpu.make_async_remote_copy(
@@ -288,14 +306,13 @@
             encode(part_sum[step, HALF:] + decode(through.at[4 + col]), coded.at[step, 1])
             high(step, 1, col).start()
 
-    def project(step):
+    def product(step):
         k, _, _, _ = where(step)
         rows = pl.ds(pl.multiple_of(k * FEA, FEA), FEA)
-        total[...] += jnp.dot(held[k, :TOK], panel[rows, :], preferred_element_type=jnp.float32)
-
-    def out_copy(col):
-        columns = pl.ds(pl.multiple_of(col * FEA, FEA), FEA)
-        return pltpu.make_async_copy(cov_buf.at[col], cov.at[:, columns], out_sem.at[col])
+        return jnp.dot(held[k, :TOK], panel[rows, :], preferred_element_type=jnp.float32)
+
+    def project(step):
+        total[...] += (product(step) + product(step + 1)) + (product(step + 2) + product(step + 3))
 
     def finish(step):
         _, col, hops, mine = where(step)
@@ -308,8 +325,8 @@
                 slot = 2 * col + half
                 rows = pl.ds(half * HALF, HALF)
                 sums = part_sum[step, rows] + (decode(from_low.at[slot]) + decode(from_high.at[slot]))
-                cov_buf[col, rows] = sums / jnp.float32(tokens)
-            out_copy(col).start()
+                columns = pl.ds(pl.multiple_of(col * FEA, FEA), FEA)
+                cov[rows, columns] = sums / jnp.float32(tokens)
 
     def sent(step):
         k, col, hops, mine = where(step)
@@ -324,6 +341,7 @@
                 low(step, half, col).wait_send()
 
     run(-1)
+    a_copy.wait()
     share(0)
     own_t[:, :TOK] = held[own, :TOK].T
     to_core(0, own).wait_recv()
@@ -343,11 +361,11 @@
         def _():
             partial(step - 1)
 
-        @pl.when(step >= LAG)
+        @pl.when((step >= LAG) & (step < STEPS + LAG))
         def _():
             pass_on(step - LAG)
 
-        @pl.when(step >= GATE_LAG)
+        @pl.when((step >= GATE_LAG) & (step % 4 == GATE_LAG % 4))
         def _():
             project(step - GATE_LAG)
 
@@ -357,10 +375,8 @@
 
         return 0
 
-    lax.fori_loop(0, STEPS + LAG, step_body, 0)
-    gate_buf[...] = total[...].astype(gate.dtype)
-    gate_copy = pltpu.make_async_copy(gate_buf, gate, a_sem)
-    gate_copy.start()
+    lax.fori_loop(0, STEPS + MOST, step_body, 0)
+    gate[...] = total[...].astype(gate.dtype)
 
     def last_body(step, _):
         finish(step)
@@ -373,10 +389,7 @@
     lax.fori_loop(0, STEPS, sent_body, 0)
     for n in range(len(SENDS)):
         gather(n).wait_send()
-    lax.fori_loop(STEPS + LAG - END_LAG, STEPS, last_body, 0)
-    gate_copy.wait()
-    for col in range(4):
-        out_copy(col).wait()
+    lax.fori_loop(STEPS + MOST - END_LAG, STEPS, last_body, 0)
 
 
 def solution(mesh):
@@ -387,11 +400,11 @@
         return pl.pallas_call(
             functools.partial(kernel, tokens),
             out_shape=(
-                jax.ShapeDtypeStruct((FEA, 4 * FEA), f32),
-                jax.ShapeDtypeStruct((TOK, HID), bf16),
+                pltpu.VMEM((FEA, 4 * FEA), f32),
+                pltpu.VMEM((TOK, HID), bf16),
             ),
             in_specs=[pl.BlockSpec(memory_space=pl.ANY)] * 2,
-            out_specs=[pl.BlockSpec(memory_space=pl.ANY)] * 2,
+            out_specs=[pl.BlockSpec(memory_space=pltpu.VMEM)] * 2,
             scratch_shapes=[
                 pltpu.VMEM((32, 2 * TOK, FEA), bf16),
                 pltpu.VMEM((FEA, 2 * TOK), bf16),
@@ -402,8 +415,6 @@
                 pltpu.VMEM((8, CODED, FEA), bf16),
                 pltpu.VMEM((8, CODED, FEA), bf16),
                 pltpu.VMEM((8, CODED, FEA), bf16),
-                pltpu.VMEM((4, FEA, FEA), f32),
-                pltpu.VMEM((TOK, HID), bf16),
                 sems((len(SENDS),)),
                 sems((len(SENDS),)),
                 sems((STEPS,)),
@@ -414,7 +425,6 @@
                 sems((8,)),
                 sems(()),
                 sems(()),
-                sems((4,)),
             ],
             compiler_params=pltpu.CompilerParams(
                 collective_id=0, has_side_effects=True, vmem_limit_bytes=56 * 2**20

time: 68.8 us -> 61.8 us (0.90)
  Pallas kernels: 63.9 us -> 59.4 us
  local copies, waits for them, and re-layouts: 4.07 us -> 1.72 us
    pallas_call x1, Pallas kernels: 63.9 us -> 59.4 us  [step(): pl.pallas_call(functools.partial(kernel, tokens), out_shape=(pltpu.VMEM((...]
    unnamed x2, local copies, waits for them, and re-layouts: 4.07 us -> 1.72 us
where the time goes in v3:
time: 61.8 us; the launch traced here: 61.7 us
  Pallas kernels  59.4 us (96%)
  local copies, waits for them, and re-layouts  1.72 us (3%)
  between operations  0.64 us (1%)
    pallas_call x1, Pallas kernels, step(): pl.pallas_call(functools.partial(kernel, tokens), out_shape=(pltpu.VMEM((...  59.4 us
    unnamed x2, local copies, waits for them, and re-layouts  1.72 us

profile of v3, /device:TPU:4, one launch (start us, length us, event | category | flops | bytes accessed | tf_op | source)
XLA Modules:
  0.0 61.7 jit_solution(15442544433409310066)
XLA Ops:
  0.6 59.4 %shard_map.41 = (f32[256,1024]{1,0:T(8,128)S(1)}, bf16[384,512]{1,0:T(8,128)(2,1)S(1)}) custom-call(bf16[384,256]{1,0:T(8,128)(2,1)} %acts.1, bf16[8192,512]{1,0:T(8,128)(2,1)} %weight.1), custom_call_target="tpu_custom_call" | custom-call | tf_op jit(solution)/shard_map/pallas_call | solution.py:400
  60.0 1.0 %copy.6 = f32[256,1024]{1,0:T(8,128)} copy(f32[256,1024]{1,0:T(8,128)S(1)} %get-tuple-element.2) | data formatting | bytes 2097152
  61.0 0.7 %copy.7 = bf16[384,512]{1,0:T(8,128)(2,1)} copy(bf16[384,512]{1,0:T(8,128)(2,1)S(1)} %get-tuple-element.3) | data formatting | bytes 786432

commit v4 on v3

--- a/solution.py
+++ b/solution.py
@@ -43,9 +43,9 @@
 PARTS = ((0, SPLIT), (SPLIT, TOK))
 STEPS = len(ORDER)
 HALF = FEA // 2
-LAG = 6
-GATE_LAG = 12
-END_LAG = 20
+LAG = 10
+GATE_LAG = 16
+END_LAG = 22
 MOST = max(LAG, GATE_LAG - 3)
 SCALE = 256 * 5.45
 CODED = HALF + HALF // 4
@@ -392,12 +392,21 @@
     lax.fori_loop(STEPS + MOST - END_LAG, STEPS, last_body, 0)
 
 
+def leave(cov_in, gate_in, cov, gate, sem):
+    one = pltpu.make_async_copy(cov_in, cov, sem.at[0])
+    two = pltpu.make_async_copy(gate_in, gate, sem.at[1])
+    one.start()
+    two.start()
+    one.wait()
+    two.wait()
+
+
 def solution(mesh):
     def step(acts, weight):
         tokens = acts.shape[0] * mesh.shape["dp"]
         sems = pltpu.SemaphoreType.DMA
         f32, bf16 = jnp.float32, jnp.bfloat16
-        return pl.pallas_call(
+        sums = pl.pallas_call(
             functools.partial(kernel, tokens),
             out_shape=(
                 pltpu.VMEM((FEA, 4 * FEA), f32),
@@ -430,6 +439,17 @@
                 collective_id=0, has_side_effects=True, vmem_limit_bytes=56 * 2**20
             ),
         )(acts, weight)
+        return pl.pallas_call(
+            leave,
+            out_shape=(
+                jax.ShapeDtypeStruct((FEA, 4 * FEA), f32),
+                jax.ShapeDtypeStruct((TOK, HID), bf16),
+            ),
+            in_specs=[pl.BlockSpec(memory_space=pltpu.VMEM)] * 2,
+            out_specs=[pl.BlockSpec(memory_space=pl.ANY)] * 2,
+            scratch_shapes=[sems((2,))],
+            compiler_params=pltpu.CompilerParams(vmem_limit_bytes=4 * 2**20),
+        )(*(pltpu.with_memory_space_constraint(s, pltpu.VMEM) for s in sums))
 
     return jax.shard_map(
         step,

time: 61.8 us -> 61.1 us (0.989)
  local copies, waits for them, and re-layouts: 1.72 us -> 0 us
  Pallas kernels: 59.4 us -> 60.4 us
    unnamed x2 -> x0, local copies, waits for them, and re-layouts: 1.72 us -> none
    pallas_call x0 -> x1, Pallas kernels: none -> 1.11 us  [step(): pl.pallas_call(leave, out_shape=(jax.ShapeDtypeStruct((FEA, 4 * FEA), f32...]
where the time goes in v4:
time: 61.1 us; the launch traced here: 61 us
  Pallas kernels  60.4 us (99%)
  between operations  0.64 us (1%)
    pallas_call x1, Pallas kernels, step(): pl.pallas_call(functools.partial(kernel, tokens), out_shape=(pltpu.VMEM((...  59.2 us

profile of v4, /device:TPU:4, one launch (start us, length us, event | category | flops | bytes accessed | tf_op | source)
XLA Modules:
  0.0 61.0 jit_solution(1158915709419332866)
XLA Ops:
  0.6 59.2 %shard_map.41 = (f32[256,1024]{1,0:T(8,128)S(1)}, bf16[384,512]{1,0:T(8,128)(2,1)S(1)}) custom-call(bf16[384,256]{1,0:T(8,128)(2,1)} %acts.1, bf16[8192,512]{1,0:T(8,128)(2,1)} %weight.1), custom_call_target="tpu_custom_call" | custom-call | tf_op jit(solution)/shard_map/pallas_call | solution.py:409
  59.9 1.1 %shard_map.42 = (f32[256,1024]{1,0:T(8,128)}, bf16[384,512]{1,0:T(8,128)(2,1)}) custom-call(f32[256,1024]{1,0:T(8,128)S(1)} %get-tuple-element.4.cov_in, bf16[384,512]{1,0:T(8,128)(2,1)S(1)} %get-tuple-element.5.gate_in), custom_call_target="tpu_custom_call" | custom-call | tf_op jit(solution)/shard_map/pallas_call | solution.py:442

commit v5 on v4

--- a/solution.py
+++ b/solution.py
@@ -45,6 +45,7 @@
 HALF = FEA // 2
 LAG = 10
 GATE_LAG = 16
+SENT_LAG = 24
 END_LAG = 22
 MOST = max(LAG, GATE_LAG - 3)
 SCALE = 256 * 5.45
@@ -208,6 +209,10 @@
         if step >= 0:
             for part in range(2):
                 want(step, needed(part, *ORDER[step], 2))
+            for n, send in enumerate(SENDS):
+                if send[0] == step - 9:
+                    events[step + 1].append((lambda m: gather(m).wait_send(), n))
+    late = [n for n, send in enumerate(SENDS) if send[0] + 9 >= STEPS]
 
     def run(step):
         for action, n in events[step + 1]:
@@ -326,7 +331,7 @@
                 rows = pl.ds(half * HALF, HALF)
                 sums = part_sum[step, rows] + (decode(from_low.at[slot]) + decode(from_high.at[slot]))
                 columns = pl.ds(pl.multiple_of(col * FEA, FEA), FEA)
-                cov[rows, columns] = sums / jnp.float32(tokens)
+                cov[rows, columns] = sums * jnp.float32(1.0 / tokens)
 
     def sent(step):
         k, col, hops, mine = where(step)
@@ -346,7 +351,6 @@
     own_t[:, :TOK] = held[own, :TOK].T
     to_core(0, own).wait_recv()
     own_t[:, TOK:] = held[own, TOK:].T
-    w_copy.wait()
 
     def step_body(step, _):
         @pl.when(step < STEPS)
@@ -367,11 +371,19 @@
 
         @pl.when((step >= GATE_LAG) & (step % 4 == GATE_LAG % 4))
         def _():
+            @pl.when(step == GATE_LAG)
+            def _():
+                w_copy.wait()
+
             project(step - GATE_LAG)
 
         @pl.when(step >= END_LAG)
         def _():
             finish(step - END_LAG)
+
+        @pl.when(step >= SENT_LAG)
+        def _():
+            sent(step - SENT_LAG)
 
         return 0
 
@@ -386,8 +398,8 @@
         sent(step)
         return 0
 
-    lax.fori_loop(0, STEPS, sent_body, 0)
-    for n in range(len(SENDS)):
+    lax.fori_loop(STEPS + MOST - SENT_LAG, STEPS, sent_body, 0)
+    for n in late:
         gather(n).wait_send()
     lax.fori_loop(STEPS + MOST - END_LAG, STEPS, last_body, 0)
 

time: 61.1 us -> 61.2 us (level)
  no operation moved by 1% of the time
where the time goes in v5:
time: 61.2 us; the launch traced here: 61.1 us
  Pallas kernels  60.5 us (99%)
  between operations  0.64 us (1%)
    pallas_call x1, Pallas kernels, step(): pl.pallas_call(functools.partial(kernel, tokens), out_shape=(pltpu.VMEM((...  59.4 us

profile of v5, /device:TPU:4, one launch (start us, length us, event | category | flops | bytes accessed | tf_op | source)
XLA Modules:
  0.0 61.1 jit_solution(4406083093198704434)
XLA Ops:
  0.6 59.4 %shard_map.41 = (f32[256,1024]{1,0:T(8,128)S(1)}, bf16[384,512]{1,0:T(8,128)(2,1)S(1)}) custom-call(bf16[384,256]{1,0:T(8,128)(2,1)} %acts.1, bf16[8192,512]{1,0:T(8,128)(2,1)} %weight.1), custom_call_target="tpu_custom_call" | custom-call | tf_op jit(solution)/shard_map/pallas_call | solution.py:421
  60.0 1.1 %shard_map.42 = (f32[256,1024]{1,0:T(8,128)}, bf16[384,512]{1,0:T(8,128)(2,1)}) custom-call(f32[256,1024]{1,0:T(8,128)S(1)} %get-tuple-element.4.cov_in, bf16[384,512]{1,0:T(8,128)(2,1)S(1)} %get-tuple-element.5.gate_in), custom_call_target="tpu_custom_call" | custom-call | tf_op jit(solution)/shard_map/pallas_call | solution.py:454
